TPU v7x, 256 devices: a whole 4x4x8 slice. The times are simulated.
256 devices in a mesh: row: 32 (over x, z_lo, core), col: 8 (over z_hi, y).
Axes of the slice: x: 4, y: 4, z: 8 (z_hi: 2, z_lo: 4; z = z_hi * 4 + z_lo), core: 2. Of those that a mesh axis runs over, the one named last changes fastest.
Arguments:
- s_band: bfloat16 [256, 65536], P(None, ('col', 'row')), may hold values from -6 to 6
- t_band: bfloat16 [256, 65536], P(None, ('col', 'row')), may hold values from -6 to 6
- q_rows: bfloat16 [4096, 65536], P('row', 'col'), may hold values from -6 to 6
- z_rows: bfloat16 [4096, 65536], P('row', 'col'), may hold values from -6 to 6
- factors: bfloat16 [16, 2, 256, 256], P(None, None, 'row', 'col'), may hold values from -0.375 to 0.375
- starts: int32 [16], replicated, may hold values from 0 to 65280, as said below
- flags: int32 [16], replicated, may hold values from 0 to 1, as said below
Outputs:
- q_out: bfloat16 [4096, 65536], P('row', 'col')
- z_out: bfloat16 [4096, 65536], P('row', 'col')
- s_out: bfloat16 [256, 65536], P(None, ('col', 'row'))
- t_out: bfloat16 [256, 65536], P(None, ('col', 'row'))
Inputs may be any that keep to these rules, and one draw needn't show every extreme that they name: The starts are distinct multiples of 256; starts[0] = 0. At most 8 windows start within the columns of one index of col, and exactly 8 do for some index. flags[0] = 1.
All inputs are finite; a program needn't handle non-finite values.
Results may differ from a plain program's by a relative error of at most 0.0013.
Values may be sent and summed in bfloat16 or wider, within the bound.
A program may use at most 64 MiB of HBM per device.

v0:
```python
import jax
import jax.numpy as jnp
from jax import lax
from jax.sharding import PartitionSpec as P

W = 256
K = 16


def take_blocks(matrix, places):
    return jax.vmap(lambda place: lax.dynamic_slice_in_dim(matrix, place, W, 1))(places)


def place_blocks(matrix, blocks, places, live):

    def write_one(slot, current_matrix):
        current = lax.dynamic_slice_in_dim(current_matrix, places[slot], W, 1)
        value = jnp.where(live[slot], blocks[slot], current)
        return lax.dynamic_update_slice_in_dim(current_matrix, value, places[slot], 1)

    return lax.fori_loop(0, places.shape[0], write_one, matrix)


def contribute(blocks, factor_piece):
    return jnp.einsum("srp,spw->srw", blocks, factor_piece, preferred_element_type=jnp.float32)


def local(s_band, t_band, q_rows, z_rows, factors, starts, flags):
    band_height, band_width = s_band.shape
    q_height, width_local = q_rows.shape
    n_row = lax.axis_size("row")
    column = lax.axis_index("col")
    row_place = lax.axis_index("row")
    offset = starts - column * width_local
    owned = (offset >= 0) & (offset < width_local) & (flags == 1)
    band_offset = starts - (column * n_row + row_place) * band_width
    band_owned = (band_offset >= 0) & (band_offset < band_width) & (flags == 1)
    slots = jnp.arange(K, dtype=jnp.int32)
    band_slots = jnp.arange(K, dtype=jnp.int32)
    live = owned[slots]
    places = jnp.clip(offset[slots], 0, width_local - W)
    band_live = band_owned[band_slots]
    band_places = jnp.clip(band_offset[band_slots], 0, band_width - W)
    left_blocks = take_blocks(q_rows, places)
    right_blocks = take_blocks(z_rows, places)
    band_blocks = jnp.concatenate(
        [take_blocks(s_band, band_places), take_blocks(t_band, band_places)], axis=1
    )
    factor_cols = lax.all_gather(factors, "col", axis=3, tiled=True)
    piece = lax.all_gather(factor_cols, "row", axis=2, tiled=True)
    picked = jnp.take(piece, slots, axis=0)
    band_picked = jnp.take(piece[:, 1], band_slots, axis=0)
    acc_left = contribute(left_blocks, picked[:, 0])
    acc_right = contribute(right_blocks, picked[:, 1])
    acc_band = contribute(band_blocks, band_picked)
    leading = piece[0, 0]
    acc_left, acc_right, acc_band, leading = (acc_left, acc_right, acc_band, leading)
    q_out = place_blocks(q_rows, acc_left.astype(q_rows.dtype), places, live)
    z_out = place_blocks(z_rows, acc_right.astype(z_rows.dtype), places, live)
    fresh_band = acc_band.astype(s_band.dtype)
    s_mid = place_blocks(s_band, fresh_band[:, :band_height], band_places, band_live)
    t_mid = place_blocks(t_band, fresh_band[:, band_height:], band_places, band_live)
    s_out = lax.dot_general(
        leading, s_mid, (((0,), (0,)), ((), ())), preferred_element_type=jnp.float32
    ).astype(s_band.dtype)
    t_out = lax.dot_general(
        leading, t_mid, (((0,), (0,)), ((), ())), preferred_element_type=jnp.float32
    ).astype(t_band.dtype)
    return (q_out, z_out, s_out, t_out)


def solution(mesh):
    in_specs = (
        P(None, ("col", "row")),
        P(None, ("col", "row")),
        P("row", "col"),
        P("row", "col"),
        P(None, None, "row", "col"),
        P(),
        P(),
    )
    out_specs = (P("row", "col"), P("row", "col"), P(None, ("col", "row")), P(None, ("col", "row")))
    return jax.shard_map(local, mesh=mesh, in_specs=in_specs, out_specs=out_specs, check_vma=False)
```

profile of v0, /device:TPU:218, one launch (start us, length us, event | category | flops | bytes accessed | tf_op | source)
XLA Modules:
  0.0 426.7 jit_solution(4903666067037326566)
XLA Ops:
  7.2 3.2 copy.69
  12.0 48.3 %all_gather.6 = bf16[16,2,8,256]{0,2,1,3:T(8,128)(2,1)S(1)} all-gather(bf16[16,2,8,32]{0,2,1,3:T(8,128)(2,1)S(1)} %copy.16), channel_id=1, replica_groups=mesh['row'=32,'col'=8] {'col'}, dimensions={3}, use_global_device_ids=true | all-gather | bytes 147456 | tf_op jit(solution)/shard_map/all_gather | solution.py:49
  60.3 1.6 copy.17
  64.2 36.7 %while.59 = (s32[]{:T(128)}, bf16[128,8192]{1,0:T(8,128)(2,1)}, s32[16,2]{0,1:T(2,128)S(1)}, bf16[16,128,256]{2,1,0:T(8,128)(2,1)S(1)}, s32[]{:T(128)}) while((s32[]{:T(128)}, bf16[128,8192]{1,0:T(8,128)(2,1)}, s32[16,2]{0,1:T(2,128)S(1)}, bf16[16,128,256]{2,1,0:T(8,128)(2,1)S(1)}, s32[]{:T(128)}) %tuple.135), condition=%wide.while_cond.1, body=%wide.while_body.1.sunk | while | flops 2 | bytes 131169 | solution.py:11
  64.8 1.6 bitcast_dynamic-update-slice_fusion.5
  67.1 1.6 bitcast_dynamic-update-slice_fusion.5
  69.4 1.6 bitcast_dynamic-update-slice_fusion.5
  71.7 1.6 bitcast_dynamic-update-slice_fusion.5
  74.0 1.6 bitcast_dynamic-update-slice_fusion.5
  76.3 1.6 bitcast_dynamic-update-slice_fusion.5
  78.6 1.6 bitcast_dynamic-update-slice_fusion.5
  80.9 1.6 bitcast_dynamic-update-slice_fusion.5
  83.2 1.6 bitcast_dynamic-update-slice_fusion.5
  85.5 1.6 bitcast_dynamic-update-slice_fusion.5
  87.8 1.6 bitcast_dynamic-update-slice_fusion.5
  90.1 1.6 bitcast_dynamic-update-slice_fusion.5
  92.4 1.6 bitcast_dynamic-update-slice_fusion.5
  94.7 1.6 bitcast_dynamic-update-slice_fusion.5
  101.0 36.1 %while.58 = (s32[]{:T(128)}, bf16[128,8192]{1,0:T(8,128)(2,1)}, s32[16,2]{0,1:T(2,128)S(1)}, bf16[16,128,256]{2,1,0:T(8,128)(2,1)S(1)}, s32[]{:T(128)}) while((s32[]{:T(128)}, bf16[128,8192]{1,0:T(8,128)(2,1)}, s32[16,2]{0,1:T(2,128)S(1)}, bf16[16,128,256]{2,1,0:T(8,128)(2,1)S(1)}, s32[]{:T(128)}) %tuple.150), condition=%wide.while_cond, body=%wide.while_body.sunk | while | flops 2 | bytes 131169 | solution.py:11
  112.9 1.6 bitcast_dynamic-update-slice_fusion.4
  115.1 1.6 bitcast_dynamic-update-slice_fusion.4
  117.4 1.6 bitcast_dynamic-update-slice_fusion.4
  121.9 1.6 bitcast_dynamic-update-slice_fusion.4
  126.4 1.6 bitcast_dynamic-update-slice_fusion.4
  137.0 5.0 %gather_fusion.2 = bf16[16,2,256,256]{3,2,1,0:T(8,128)(2,1)} fusion(bf16[16,2,256,256]{3,2,1,0:T(8,128)(2,1)} %all-gather.2.cloned.1.call-done, s32[1024]{0:T(1024)S(1)} %pad_clamp_fusion), kind=kCustom, calls=%fused_computation.2 | custom fusion | bytes 8388672 | tf_op jit(solution)/shard_map/jit(_take)/gather | solution.py:51
  142.0 2.6 copy_select_fusion
  146.7 101.4 %while.55 = (s32[]{:T(128)}, bf16[128,8192]{1,0:T(8,128)(2,1)}, pred[16]{0:T(512)(128)(4,1)S(1)}, bf16[16,128,256]{2,1,0:T(8,128)(2,1)S(1)}, s32[16]{0:T(128)S(1)}, /*index=5*/s32[]{:T(128)}, s32[]{:T(128)}, s32[]{:T(128)}) while((s32[]{:T(128)}, bf16[128,8192]{1,0:T(8,128)(2,1)}, pred[16]{0:T(512)(128)(4,1)S(1)}, ...), condition=%wide.region_3.4_spmd, body=%wide.region_2.3_spmd.sunk | while | flops 32773 | bytes 327830 | solution.py:21
  149.8 1.6 bitcast_select_fusion.9
  156.1 1.6 bitcast_select_fusion.9
  162.5 1.6 bitcast_select_fusion.9
  168.8 1.6 bitcast_select_fusion.9
  175.2 1.6 bitcast_select_fusion.9
  181.5 1.6 bitcast_select_fusion.9
  187.9 1.6 bitcast_select_fusion.9
  194.2 1.6 bitcast_select_fusion.9
  200.6 1.6 bitcast_select_fusion.9
  206.9 1.6 bitcast_select_fusion.9
  213.2 1.6 bitcast_select_fusion.9
  219.6 1.6 bitcast_select_fusion.9
  225.9 1.6 bitcast_select_fusion.9
  232.3 1.6 bitcast_select_fusion.9
  238.6 1.6 bitcast_select_fusion.9
  248.1 2.0 fusion.11
  250.1 101.4 %while.54 = (s32[]{:T(128)}, bf16[128,8192]{1,0:T(8,128)(2,1)}, pred[16]{0:T(512)(128)(4,1)S(1)}, bf16[16,128,256]{2,1,0:T(8,128)(2,1)S(1)}, s32[16]{0:T(128)S(1)}, /*index=5*/s32[]{:T(128)}, s32[]{:T(128)}, s32[]{:T(128)}) while((s32[]{:T(128)}, bf16[128,8192]{1,0:T(8,128)(2,1)}, pred[16]{0:T(512)(128)(4,1)S(1)}, ...), condition=%wide.region_1.2_spmd, body=%wide.region_0.1_spmd.sunk | while | flops 32773 | bytes 327830 | solution.py:21
  253.3 1.6 bitcast_select_fusion.8
  259.6 1.6 bitcast_select_fusion.8
  265.9 1.6 bitcast_select_fusion.8
  272.3 1.6 bitcast_select_fusion.8
  278.6 1.6 bitcast_select_fusion.8
  285.0 1.6 bitcast_select_fusion.8
  291.3 1.6 bitcast_select_fusion.8
  297.7 1.6 bitcast_select_fusion.8
  304.0 1.6 bitcast_select_fusion.8
  310.4 1.6 bitcast_select_fusion.8
  316.7 1.6 bitcast_select_fusion.8
  323.0 1.6 bitcast_select_fusion.8
  329.4 1.6 bitcast_select_fusion.8
  335.7 1.6 bitcast_select_fusion.8
  342.1 1.6 bitcast_select_fusion.8
  351.5 1.7 slice_bitcast_fusion
  353.3 2.0 gather_fusion.4
  358.5 1.7 fusion.18
  360.2 35.1 %while.56 = (s32[]{:T(128)}, bf16[256,256]{1,0:T(8,128)(2,1)S(1)}, pred[16]{0:T(512)(128)(4,1)S(1)}, bf16[16,256,256]{2,1,0:T(8,128)(2,1)}, s32[]{:T(128)}) while((s32[]{:T(128)}, bf16[256,256]{1,0:T(8,128)(2,1)S(1)}, pred[16]{0:T(512)(128)(4,1)S(1)}, bf16[16,256,256]{2,1,0:T(8,128)(2,1)}, s32[]{:T(128)}) %tuple.141), condition=%wide.region_5.6_spmd, body=%wide.region_4.5_spmd.sunk | while | flops 65538 | bytes 393288 | solution.py:21
  397.2 20.7 %while.57 = (s32[]{:T(128)}, bf16[256,256]{1,0:T(8,128)(2,1)S(1)}, pred[16]{0:T(512)(128)(4,1)S(1)}, bf16[16,256,256]{2,1,0:T(8,128)(2,1)S(1)}, s32[]{:T(128)}) while((s32[]{:T(128)}, bf16[256,256]{1,0:T(8,128)(2,1)S(1)}, pred[16]{0:T(512)(128)(4,1)S(1)}, bf16[16,256,256]{2,1,0:T(8,128)(2,1)S(1)}, s32[]{:T(128)}) %tuple.151), condition=%wide.region_7.8_spmd, body=%wide.region_6.7_spmd.sunk | while | flops 65538 | bytes 393288 | solution.py:21
  (282 shorter events, 200.7 us)
Async XLA Ops:
  7.2 3.3 copy-start.1
  7.2 129.9 %all-gather.2.cloned.1.call-start = ((), (), s32[]{:S(2)}) async-start(), calls=%async_computation | async-start | bytes 4325376 | tf_op jit(solution)/shard_map/all_gather | solution.py:50
  10.5 1.3 copy-start.3
  10.5 1.4 copy-start.4
  10.5 1.4 copy-start.5
  11.8 50.2 %copy-start.6 = (s32[16]{0:T(128)S(1)}, s32[16]{0:T(128)}, u32[]{:S(2)}) copy-start(s32[16]{0:T(128)} %param.21) | copy-start | bytes 196
  11.8 50.2 %copy-start.7 = (s32[16]{0:T(128)S(1)}, s32[16]{0:T(128)}, u32[]{:S(2)}) copy-start(s32[16]{0:T(128)} %param.20) | copy-start | bytes 196
  144.7 2.0 copy-start
  355.3 1.6 copy-start.2
Sparse Core Ops, SparseCore 0:
  62.1 69.0 all-gather.1
where the time goes:
time: 433 us; the launch traced here: 427 us
  local copies, waits for them, and re-layouts  203 us (47%)
  other arithmetic  91.2 us (21%)
  loops' own time  63.7 us (15%)
  blocking collectives  48.3 us (11%)
  between operations  14.3 us (3%)
  matrix products  6.33 us (1%)
    select_n x64, other arithmetic, write_one(): value = jnp.where(live[slot], blocks[slot], current)  88.5 us
    gather x96, local copies, waits for them, and re-layouts  72.1 us
    another operation x4, loops' own time, place_blocks(): return lax.fori_loop(0, places.shape[0], write_one, matrix)  63 us
    dynamic_update_slice x32, local copies, waits for them, and re-layouts, write_one(): lax.dynamic_update_slice_in_dim(current_matrix, value, places[slot], 1)  50.7 us
    all_gather x1, blocking collectives, local(): factor_cols = lax.all_gather(factors, 'col', axis=3, tiled=True)  48.3 us
    dynamic_slice x64, local copies, waits for them, and re-layouts, write_one(): value = jnp.where(live[slot], blocks[slot], current)  37.7 us
    dynamic_slice x32, local copies, waits for them, and re-layouts, write_one(): current = lax.dynamic_slice_in_dim(current_matrix, places[slot], W, 1)  18.6 us
    unnamed x25, local copies, waits for them, and re-layouts  9.2 us
  transfers between devices with their start and end apart: 1, of which 0 were waited for; matrix products, arithmetic and copies ran while one was open for 17% of the time, Pallas kernels for 0%

commit v1 on v0

--- a/solution.py
+++ b/solution.py
@@ -47,7 +47,9 @@
         [take_blocks(s_band, band_places), take_blocks(t_band, band_places)], axis=1
     )
     factor_cols = lax.all_gather(factors, "col", axis=3, tiled=True)
-    piece = lax.all_gather(factor_cols, "row", axis=2, tiled=True)
+    piece = jnp.concatenate(
+        lax.all_to_all(jnp.stack([factor_cols] * lax.axis_size("row")), "row", 0, 0), axis=2
+    )
     picked = jnp.take(piece, slots, axis=0)
     band_picked = jnp.take(piece[:, 1], band_slots, axis=0)
     acc_left = contribute(left_blocks, picked[:, 0])

time: 433 us -> 453 us (1.046)
  the two profiles are of different devices: /device:TPU:218 before, /device:TPU:8 now
where the time goes in v1:
time: 453 us; the launch traced here: 446 us
  local copies, waits for them, and re-layouts  209 us (46%)
  other arithmetic  88 us (19%)
  loops' own time  61.6 us (14%)
  blocking collectives  49.2 us (11%)
  waiting for transfers between devices  21.9 us (5%)
  matrix products  8.56 us (2%)
  starting transfers between devices  6.92 us (2%)
    select_n x64, other arithmetic, write_one(): value = jnp.where(live[slot], blocks[slot], current)  87.5 us
    gather x96, local copies, waits for them, and re-layouts  70.5 us
    another operation x4, loops' own time, place_blocks(): return lax.fori_loop(0, places.shape[0], write_one, matrix)  60.9 us
    dynamic_update_slice x32, local copies, waits for them, and re-layouts, write_one(): lax.dynamic_update_slice_in_dim(current_matrix, value, places[slot], 1)  49.4 us
    all_gather x1, blocking collectives, local(): factor_cols = lax.all_gather(factors, 'col', axis=3, tiled=True)  49.2 us
    dynamic_slice x64, local copies, waits for them, and re-layouts, write_one(): value = jnp.where(live[slot], blocks[slot], current)  38.9 us
    all_to_all x1, waiting for transfers between devices, local(): lax.all_to_all(jnp.stack([factor_cols] * lax.axis_size('row')), 'row', 0, 0)  21.9 us
    dynamic_slice x32, local copies, waits for them, and re-layouts, write_one(): current = lax.dynamic_slice_in_dim(current_matrix, places[slot], W, 1)  19.8 us
  transfers between devices with their start and end apart: 1, of which 1 were waited for; matrix products, arithmetic and copies ran while one was open for 16% of the time, Pallas kernels for 0%

profile of v1, /device:TPU:8, one launch (start us, length us, event | category | flops | bytes accessed | tf_op | source)
XLA Modules:
  0.0 446.1 jit_solution(1710021024055678501)
XLA Ops:
  0.6 3.2 copy.72
  5.5 49.2 %all_gather.3 = bf16[16,2,8,256]{0,2,1,3:T(8,128)(2,1)S(1)} all-gather(bf16[16,2,8,32]{0,2,1,3:T(8,128)(2,1)S(1)} %copy.16), channel_id=1, replica_groups=mesh['row'=32,'col'=8] {'col'}, dimensions={3}, use_global_device_ids=true | all-gather | bytes 147456 | tf_op jit(solution)/shard_map/all_gather | solution.py:49
  55.7 2.4 stack.2
  58.1 6.9 %all-to-all-start = ((bf16[32,16,2,8,256]{4,3,2,1,0:T(8,128)(2,1)}), bf16[32,16,2,8,256]{4,3,2,1,0:T(8,128)(2,1)}, u32[]{:S(2)}, u32[]{:S(2)}) async-start(bf16[32,16,2,8,256]{4,3,2,1,0:T(8,128)(2,1)} %stack.2), calls=%async_computation | async-start | bytes 8388608 | tf_op jit(solution)/shard_map/all_to_all | solution.py:51
  67.2 36.8 %while.59 = (s32[]{:T(128)}, bf16[128,8192]{1,0:T(8,128)(2,1)}, s32[16,2]{0,1:T(2,128)S(1)}, bf16[16,128,256]{2,1,0:T(8,128)(2,1)S(1)}, s32[]{:T(128)}) while((s32[]{:T(128)}, bf16[128,8192]{1,0:T(8,128)(2,1)}, s32[16,2]{0,1:T(2,128)S(1)}, bf16[16,128,256]{2,1,0:T(8,128)(2,1)S(1)}, s32[]{:T(128)}) %tuple.135), condition=%wide.while_cond.1, body=%wide.while_body.1.sunk | while | flops 2 | bytes 131169 | solution.py:11
  67.9 1.7 bitcast_dynamic-update-slice_fusion.5
  70.3 1.7 bitcast_dynamic-update-slice_fusion.5
  72.6 1.7 bitcast_dynamic-update-slice_fusion.5
  74.9 1.7 bitcast_dynamic-update-slice_fusion.5
  77.3 1.6 bitcast_dynamic-update-slice_fusion.5
  79.6 1.6 bitcast_dynamic-update-slice_fusion.5
  81.8 1.6 bitcast_dynamic-update-slice_fusion.5
  84.1 1.6 bitcast_dynamic-update-slice_fusion.5
  86.4 1.6 bitcast_dynamic-update-slice_fusion.5
  88.7 1.6 bitcast_dynamic-update-slice_fusion.5
  91.0 1.6 bitcast_dynamic-update-slice_fusion.5
  93.3 1.6 bitcast_dynamic-update-slice_fusion.5
  95.6 1.6 bitcast_dynamic-update-slice_fusion.5
  97.8 1.6 bitcast_dynamic-update-slice_fusion.5
  100.1 1.6 bitcast_dynamic-update-slice_fusion.5
  102.4 1.6 bitcast_dynamic-update-slice_fusion.5
  104.2 34.4 %while.58 = (s32[]{:T(128)}, bf16[128,8192]{1,0:T(8,128)(2,1)}, s32[16,2]{0,1:T(2,128)S(1)}, bf16[16,128,256]{2,1,0:T(8,128)(2,1)S(1)}, s32[]{:T(128)}) while((s32[]{:T(128)}, bf16[128,8192]{1,0:T(8,128)(2,1)}, s32[16,2]{0,1:T(2,128)S(1)}, bf16[16,128,256]{2,1,0:T(8,128)(2,1)S(1)}, s32[]{:T(128)}) %tuple.148), condition=%wide.while_cond, body=%wide.while_body.sunk | while | flops 2 | bytes 131169 | solution.py:11
  138.5 21.9 %all-to-all-done = bf16[32,16,2,8,256]{4,3,2,1,0:T(8,128)(2,1)} async-done(((bf16[32,16,2,8,256]{4,3,2,1,0:T(8,128)(2,1)}), bf16[32,16,2,8,256]{4,3,2,1,0:T(8,128)(2,1)}, u32[]{:S(2)}, u32[]{:S(2)}) %all-to-all-start) | async-done | bytes 4194336 | tf_op jit(solution)/shard_map/all_to_all | solution.py:51
  160.4 4.6 %copy.24 = bf16[32,16,2,8,256]{4,3,0,2,1:T(8,128)(2,1)} copy(bf16[32,16,2,8,256]{4,3,2,1,0:T(8,128)(2,1)} %all-to-all-done) | data formatting | bytes 8388608 | tf_op jit(solution)/shard_map/all_to_all | solution.py:51
  165.1 5.0 %gather_fusion.2 = bf16[16,2,256,256]{3,2,1,0:T(8,128)(2,1)} fusion(bf16[16,2,256,256]{3,2,1,0:T(8,128)(2,1)} %bitcast.79, s32[1024]{0:T(1024)S(1)} %pad_clamp_fusion), kind=kCustom, calls=%fused_computation.2 | custom fusion | bytes 8388672 | tf_op jit(solution)/shard_map/jit(_take)/gather | solution.py:53
  170.1 1.9 slice_bitcast_fusion
  174.1 1.6 fusion.12
  175.7 98.7 %while.55 = (s32[]{:T(128)}, bf16[128,8192]{1,0:T(8,128)(2,1)}, pred[16]{0:T(512)(128)(4,1)S(1)}, bf16[16,128,256]{2,1,0:T(8,128)(2,1)}, s32[16]{0:T(128)S(1)}, /*index=5*/s32[]{:T(128)}, s32[]{:T(128)}, s32[]{:T(128)}) while((s32[]{:T(128)}, bf16[128,8192]{1,0:T(8,128)(2,1)}, pred[16]{0:T(512)(128)(4,1)S(1)}, ...), condition=%wide.region_3.4_spmd, body=%wide.region_2.3_spmd.sunk | while | flops 32773 | bytes 327830 | solution.py:21
  178.7 1.6 bitcast_select_fusion.9
  180.3 1.6 dynamic_update_slice.23
  185.0 1.6 bitcast_select_fusion.9
  186.6 1.6 dynamic_update_slice.23
  191.2 1.6 bitcast_select_fusion.9
  192.8 1.6 dynamic_update_slice.23
  197.4 1.6 bitcast_select_fusion.9
  199.0 1.6 dynamic_update_slice.23
  274.4 3.1 fusion.11
  277.6 101.9 %while.54 = (s32[]{:T(128)}, bf16[128,8192]{1,0:T(8,128)(2,1)}, pred[16]{0:T(512)(128)(4,1)S(1)}, bf16[16,128,256]{2,1,0:T(8,128)(2,1)}, s32[16]{0:T(128)S(1)}, /*index=5*/s32[]{:T(128)}, s32[]{:T(128)}, s32[]{:T(128)}) while((s32[]{:T(128)}, bf16[128,8192]{1,0:T(8,128)(2,1)}, pred[16]{0:T(512)(128)(4,1)S(1)}, ...), condition=%wide.region_1.2_spmd, body=%wide.region_0.1_spmd.sunk | while | flops 32773 | bytes 327830 | solution.py:21
  280.8 1.6 bitcast_select_fusion.8
  282.4 1.6 dynamic_update_slice.22
  287.2 1.6 bitcast_select_fusion.8
  288.8 1.6 dynamic_update_slice.22
  293.6 1.6 bitcast_select_fusion.8
  295.3 1.6 dynamic_update_slice.22
  300.1 1.6 bitcast_select_fusion.8
  301.7 1.6 dynamic_update_slice.22
  306.5 1.6 bitcast_select_fusion.8
  312.9 1.6 bitcast_select_fusion.8
  319.2 1.6 bitcast_select_fusion.8
  325.6 1.6 bitcast_select_fusion.8
  331.9 1.6 bitcast_select_fusion.8
  338.3 1.6 bitcast_select_fusion.8
  344.6 1.6 bitcast_select_fusion.8
  351.0 1.6 bitcast_select_fusion.8
  357.3 1.6 bitcast_select_fusion.8
  363.7 1.6 bitcast_select_fusion.8
  370.0 1.6 bitcast_select_fusion.8
  376.4 1.6 bitcast_select_fusion.8
  379.5 2.0 gather_fusion.4
  383.1 1.6 fusion.4
  384.7 1.7 fusion.18
  386.5 35.1 %while.56 = (s32[]{:T(128)}, bf16[256,256]{1,0:T(8,128)(2,1)S(1)}, pred[16]{0:T(512)(128)(4,1)S(1)}, bf16[16,256,256]{2,1,0:T(8,128)(2,1)}, s32[]{:T(128)}) while((s32[]{:T(128)}, bf16[256,256]{1,0:T(8,128)(2,1)S(1)}, pred[16]{0:T(512)(128)(4,1)S(1)}, bf16[16,256,256]{2,1,0:T(8,128)(2,1)}, s32[]{:T(128)}) %tuple.141), condition=%wide.region_5.6_spmd, body=%wide.region_4.5_spmd.sunk | while | flops 65538 | bytes 393288 | solution.py:21
  417.8 1.6 bitcast_select_fusion.10
  423.5 20.7 %while.57 = (s32[]{:T(128)}, bf16[256,256]{1,0:T(8,128)(2,1)S(1)}, pred[16]{0:T(512)(128)(4,1)S(1)}, bf16[16,256,256]{2,1,0:T(8,128)(2,1)S(1)}, s32[]{:T(128)}) while((s32[]{:T(128)}, bf16[256,256]{1,0:T(8,128)(2,1)S(1)}, pred[16]{0:T(512)(128)(4,1)S(1)}, bf16[16,256,256]{2,1,0:T(8,128)(2,1)S(1)}, s32[]{:T(128)}) %tuple.149), condition=%wide.region_7.8_spmd, body=%wide.region_6.7_spmd.sunk | while | flops 65538 | bytes 393288 | solution.py:21
  (289 shorter events, 205.9 us)
Async XLA Ops:
  0.6 3.3 copy-start.4
  3.9 1.3 copy-start.6
  3.9 1.3 copy-start.7
  3.9 1.4 copy-start.8
  58.1 7.0 %copy-start.9 = (s32[16]{0:T(128)S(1)}, s32[16]{0:T(128)}, u32[]{:S(2)}) copy-start(s32[16]{0:T(128)} %param.21) | copy-start | bytes 196
  58.1 7.0 %copy-start.10 = (s32[16]{0:T(128)S(1)}, s32[16]{0:T(128)}, u32[]{:S(2)}) copy-start(s32[16]{0:T(128)} %param.20) | copy-start | bytes 196
  58.1 102.3 %all-to-all-start = ((bf16[32,16,2,8,256]{4,3,2,1,0:T(8,128)(2,1)}), bf16[32,16,2,8,256]{4,3,2,1,0:T(8,128)(2,1)}, u32[]{:S(2)}, u32[]{:S(2)}) async-start(bf16[32,16,2,8,256]{4,3,2,1,0:T(8,128)(2,1)} %stack.2), calls=%async_computation | async-start | bytes 8388608 | tf_op jit(solution)/shard_map/all_to_all | solution.py:51
  104.0 61.0 %copy-start.2 = (bf16[16,128,256]{2,1,0:T(8,128)(2,1)}, bf16[16,128,256]{2,1,0:T(8,128)(2,1)S(1)}, u32[]{:S(2)}) copy-start(bf16[16,128,256]{2,1,0:T(8,128)(2,1)S(1)} %get-tuple-element.391) | copy-start | bytes 3145732
  170.0 2.8 copy-start.1
  172.9 1.2 copy-start.3
  173.3 2.4 copy-start
  381.5 1.6 copy-start.5
